TPU v7x, 512 devices: a whole 4x8x8 slice. The times are simulated.
512 devices in a mesh: row: 16 (over y, core), col: 32 (over x, z).
Axes of the slice: x: 4, y: 8, z: 8, core: 2. Of those that a mesh axis runs over, the one named last changes fastest.
Arguments:
- lam: float32 [14400, 2400], P('row', 'col'), may hold values from -6 to 6
- cycle: float32 [2400, 24000], P('row', 'col'), may hold values from -0.125 to 0.125
- eps_occ: float32 [200], replicated, may hold values from -2 to -0.3
- eps_vir: float32 [1200], replicated, may hold values from 0.1 to 3
- occ_irrep: int32 [200], replicated, may hold values from 0 to 7
- slab: int32 [12], replicated, may hold values from 0 to 199, as said below
- pair_occ: int32 [20], replicated, may hold values from 0 to 199, as said below
- irrep_start: int32 [8], replicated, may hold values from 0 to 1125, as said below
Outputs:
- update: float32 [14400, 24000], P('row', 'col')
Inputs may be any that keep to these rules, and one draw needn't show every extreme that they name: `irrep_start`: entry 0 is 0 and the entries rise strictly, so each irrep holds one or more virtual orbitals; the last entry is 1125; sizes may differ. `slab`: distinct occupied orbitals. `pair_occ`: distinct occupied orbitals.
All inputs are finite; a program needn't handle non-finite values.
Results may differ from a plain program's by a relative error of at most 0.000073.
Values sent between devices are 32-bit elements; how exact they have to be, the bound alone decides.
A program may use at most 128 MiB of HBM per device.

v0:
```python
import jax
import jax.numpy as jnp
from jax import lax
from jax.sharding import PartitionSpec as P

V = 1200


def irrep_of(index, starts):
    return jnp.sum((index[:, None] >= starts[None, :]).astype(jnp.int32), axis=1) - 1


def local(lam, cycle, eps_occ, eps_vir, occ_irrep, slab, pair_occ, irrep_start):
    row_count = lam.shape[0]
    col_count = cycle.shape[1]
    cycle_full = lax.all_gather(cycle, "row", axis=0, tiled=True)
    prod = jnp.dot(
        lax.all_gather(lam, "col", axis=1, tiled=True),
        cycle_full,
        precision=lax.Precision.HIGHEST,
        preferred_element_type=jnp.float32,
    )
    rows = lax.axis_index("row") * row_count + jnp.arange(row_count, dtype=jnp.int32)
    cols = lax.axis_index("col") * col_count + jnp.arange(col_count, dtype=jnp.int32)
    occ_row = jnp.take(slab, rows // V)
    vir_row = rows % V
    occ_col = jnp.take(pair_occ, cols // V)
    vir_col = cols % V
    row_energy = jnp.take(eps_occ, occ_row) - jnp.take(eps_vir, vir_row)
    col_energy = jnp.take(eps_occ, occ_col) - jnp.take(eps_vir, vir_col)
    row_sym = jnp.bitwise_xor(jnp.take(occ_irrep, occ_row), irrep_of(vir_row, irrep_start))
    col_sym = jnp.bitwise_xor(jnp.take(occ_irrep, occ_col), irrep_of(vir_col, irrep_start))
    allowed = row_sym[:, None] == col_sym[None, :]
    denom = row_energy[:, None] + col_energy[None, :]
    return jnp.where(allowed, prod / denom, jnp.float32(0.0))


def solution(mesh):
    placed = (P("row", "col"), P("row", "col"), P(), P(), P(), P(), P(), P())
    return jax.shard_map(
        local, mesh=mesh, in_specs=placed, out_specs=P("row", "col"), check_vma=False
    )
```

profile of v0, /device:TPU:1, one launch (start us, length us, event | category | flops | bytes accessed | tf_op | source)
XLA Modules:
  0.0 253.9 jit_solution(11986677601947028953)
XLA Ops:
  6.5 0.0 copy-start
  6.5 0.0 copy-start.1
  6.5 0.0 copy-start.2
  6.5 0.0 all-gather.7.cloned.1.call-start
  6.5 0.7 all-gather.7.cloned.1.call-update
  7.3 0.0 all-gather.5.cloned.1.call-start
  7.3 0.7 all-gather.5.cloned.1.call-update
  8.0 1.3 slice.33
  9.3 0.1 compare_reduce_fusion.5
  9.4 0.1 compare_reduce_fusion.7
  9.4 0.1 compare_reduce_fusion.9
  9.5 0.1 compare_reduce_fusion.11
  9.5 0.1 compare_reduce_fusion.13
  9.6 0.1 compare_reduce_fusion.15
  9.6 2.1 fusion.16
  11.7 4.4 %fusion.11 = (s32[750]{0:T(1024)S(1)}, s32[750]{0:T(1024)S(1)}) fusion(s32[]{:T(128)} %bitcast.28, s32[]{:T(128)} %bitcast.29, s32[]{:T(128)} %bitcast.30, s32[]{:T(128)} %bitcast.31, s32[]{:T(128)} %bitcast.32, s32[]{:T(128)} %bitcast.34, s32[]{:T(128)} %bitcast.33, s32[]{:T(128)S(6)} %mul.7), kind=kLoop, calls=%fused_computation.89 | loop fusion | flops 23250 | bytes 6032 | tf_op jit(solution)/shard_map/jit(_take)/gather | solution.py:27
  16.2 8.2 %select_select_fusion = s32[750]{0:T(1024)S(1)} fusion(pred[750]{0:T(1024)(128)(4,1)S(1)} %get-tuple-element.36, pred[750]{0:T(1024)(128)(4,1)S(1)} %get-tuple-element.37, pred[750]{0:T(1024)(128)(4,1)S(1)} %get-tuple-element.38, pred[750]{0:T(1024)(128)(4,1)S(1)} %get-tuple-element.39, pred[750]{0:T(1024)(128)(4,1)S(1)} %get-tuple-element.40, ...), kind=kLoop, calls=%fused_computation.65 | loop fusion | flops 9750 | bytes 15802 | tf_op jit(solution)/shard_map/jit(_take)/gather | solution.py:27
  24.4 4.8 %gather_fusion.4 = f32[750]{0:T(1024)S(1)} fusion(f32[200]{0:T(256)} %param.10, s32[1024]{0:T(1024)S(1)} %pad_clamp_fusion.2), kind=kCustom, calls=%fused_computation.4 | custom fusion | bytes 9000 | tf_op jit(solution)/shard_map/jit(_take)/gather | solution.py:30
  29.2 0.1 compare_reduce_fusion
  29.3 0.1 compare_reduce_fusion.1
  29.3 0.1 compare_reduce_fusion.2
  29.4 0.1 compare_reduce_fusion.3
  29.4 0.1 compare_reduce_fusion.4
  29.5 1.8 fusion.15
  31.3 4.5 %compare_select_fusion.6 = s32[900,1]{0,1:T(1,128)S(1)} fusion(s32[]{:T(128)} %bitcast.5, s32[]{:T(128)} %bitcast.6, s32[]{:T(128)} %bitcast.7, s32[]{:T(128)} %bitcast.8, s32[]{:T(128)} %bitcast.9, s32[]{:T(128)} %bitcast.11, s32[]{:T(128)} %bitcast.10, s32[]{:T(128)S(6)} %mul.6), kind=kLoop, calls=%fused_computation.20 | loop fusion | flops 21600 | bytes 3632 | tf_op jit(solution)/shard_map/jit(_take)/gather | solution.py:25
  35.7 3.1 %select_select_fusion.1 = s32[900]{0:T(1024)S(1)} fusion(pred[900]{0:T(1024)(128)(4,1)S(1)} %compare_reduce_fusion, pred[900]{0:T(1024)(128)(4,1)S(1)} %compare_reduce_fusion.1, pred[900]{0:T(1024)(128)(4,1)S(1)} %compare_reduce_fusion.2, pred[900]{0:T(1024)(128)(4,1)S(1)} %compare_reduce_fusion.3, pred[900]{0:T(1024)(128)(4,1)S(1)} %compare_reduce_fusion.4, ...), kind=kLoop, calls=%fused_computation.66 | loop fusion | flops 4500 | bytes 11720 | tf_op jit(solution)/shard_map/jit(_take)/gather | solution.py:25
  38.8 0.1 compare_select_fusion
  38.9 0.0 copy-done.1
  38.9 6.5 %gather_fusion.2 = f32[900]{0:T(1024)S(1)} fusion(f32[200]{0:T(256)S(1)} %copy-done.1, s32[1024]{0:T(1024)S(1)} %pad_clamp_fusion.3), kind=kCustom, calls=%fused_computation.2 | custom fusion | bytes 10800 | tf_op jit(solution)/shard_map/jit(_take)/gather | solution.py:29
  45.4 0.0 copy-done.2
  45.4 0.0 copy-start.3
  45.4 5.0 %gather_fusion.1 = s32[750]{0:T(1024)S(1)} fusion(s32[200]{0:T(256)S(1)} %copy-done.2, s32[1024]{0:T(1024)S(1)} %pad_clamp_fusion.2), kind=kCustom, calls=%fused_computation.1 | custom fusion | bytes 9000 | tf_op jit(solution)/shard_map/jit(_take)/gather | solution.py:32
  50.4 6.5 %gather_fusion = s32[900]{0:T(1024)S(1)} fusion(s32[200]{0:T(256)S(1)} %copy-done.2, s32[1024]{0:T(1024)S(1)} %pad_clamp_fusion.3), kind=kCustom, calls=%fused_computation | custom fusion | bytes 10800 | tf_op jit(solution)/shard_map/jit(_take)/gather | solution.py:31
  56.9 0.0 copy-done
  56.9 4.5 %gather_fusion.5 = f32[750]{0:T(1024)S(1)} fusion(f32[1200]{0:T(1024)S(1)} %copy-done, s32[1024]{0:T(1024)S(1)} %pad_clamp_fusion), kind=kCustom, calls=%fused_computation.5 | custom fusion | bytes 9000 | tf_op jit(solution)/shard_map/jit(_take)/gather | solution.py:30
  61.4 5.9 %gather_fusion.3 = f32[900]{0:T(1024)S(1)} fusion(f32[1200]{0:T(1024)S(1)} %copy-done, s32[1024]{0:T(1024)S(1)} %pad_clamp_fusion.1), kind=kCustom, calls=%fused_computation.3 | custom fusion | bytes 10800 | tf_op jit(solution)/shard_map/jit(_take)/gather | solution.py:29
  67.3 0.0 copy-done.3
  67.3 0.1 convert_reduce_fusion.1
  67.4 0.1 convert_reduce_fusion
  67.6 1.7 all-gather.7.cloned.1.call-done
  69.3 6.8 %reshape.467 = f32[2400,750]{1,0:T(8,128)} reshape(f32[16,150,750]{2,1,0:T(8,128)} %all-gather.7.cloned.1.call-done) | data formatting | bytes 14400000
  76.1 109.9 %all-gather.5.cloned.1.call-done = f32[32,75,900]{2,1,0:T(8,128)} async-done(((f32[1,75,900]{2,1,0:T(8,128)}), f32[32,75,900]{2,1,0:T(8,128)}) %all-gather.5.cloned.1.call-update) | async-done | bytes 8640016 | tf_op jit(solution)/shard_map/all_gather | solution.py:18
  186.0 8.2 %reshape.465 = f32[2400,900]{1,0:T(8,128)} reshape(f32[32,75,900]{2,1,0:T(8,128)} %all-gather.5.cloned.1.call-done) | data formatting | bytes 17280000
  194.3 52.8 %divide_select_fusion = f32[900,750]{1,0:T(8,128)} fusion(f32[2400,900]{1,0:T(8,128)} %reshape.465, f32[2400,750]{1,0:T(8,128)} %reshape.467, f32[750]{0:T(1024)S(1)} %select_subtract_fusion, f32[900]{0:T(1024)S(1)} %select_subtract_fusion.1, s32[750]{0:T(1024)S(1)} %add_xor_fusion, s32[900]{0:T(1024)S(1)} %add_xor_fusion.1), kind=kOutput, calls=%fused_computation.6 | convolution fusion | flops 19442702336 | bytes 18553200 | tf_op jit(solution)/shard_map/dot_general | solution.py:17
  (12 shorter events, 0.2 us)
Async XLA Ops:
  6.5 50.4 %copy-start = (f32[1200]{0:T(1024)S(1)}, f32[1200]{0:T(1024)}, u32[]{:S(2)}) copy-start(f32[1200]{0:T(1024)} %param.11) | copy-start | bytes 14404
  6.5 32.3 %copy-start.1 = (f32[200]{0:T(256)S(1)}, f32[200]{0:T(256)}, u32[]{:S(2)}) copy-start(f32[200]{0:T(256)} %param.10) | copy-start | bytes 2404
  6.5 38.9 %copy-start.2 = (s32[200]{0:T(256)S(1)}, s32[200]{0:T(256)}, u32[]{:S(2)}) copy-start(s32[200]{0:T(256)} %param.12) | copy-start | bytes 2404
  6.5 62.8 %all-gather.7.cloned.1.call-start = ((), (), s32[]{:S(2)}) async-start(), calls=%async_computation.1 | async-start | bytes 7938048 | tf_op jit(solution)/shard_map/all_gather | solution.py:16
  7.3 178.8 %all-gather.5.cloned.1.call-start = ((), (), s32[]{:S(2)}) async-start(), calls=%async_computation | async-start | bytes 10813440 | tf_op jit(solution)/shard_map/all_gather | solution.py:18
  45.4 21.9 %copy-start.3 = (s32[8]{0:T(128)S(1)}, s32[8]{0:T(128)}, u32[]{:S(2)}) copy-start(s32[8]{0:T(128)} %param.15) | copy-start | bytes 100
Sparse Core Ops, SparseCore 0:
  9.5 59.7 all-gather.6
  72.5 113.4 all-gather.4
where the time goes:
time: 254 us
  waiting for transfers between devices  113 us (44%)
  local copies, waits for them, and re-layouts  53.2 us (21%)
  matrix products  52.8 us (21%)
  other arithmetic  21.1 us (8%)
  between operations  13.6 us (5%)
    all_gather x1, waiting for transfers between devices, local(): lax.all_gather(lam, 'col', axis=1, tiled=True)  110 us
    dot_general x1, matrix products, local(): jnp.dot(lax.all_gather(lam, 'col', axis=1, tiled=True), cycle_full, preci...  52.8 us
    unnamed x10, local copies, waits for them, and re-layouts  15 us
    gather x9, other arithmetic, local(): occ_col = jnp.take(pair_occ, cols // V)  12.9 us
    gather x2, local copies, waits for them, and re-layouts, local(): row_energy = jnp.take(eps_occ, occ_row) - jnp.take(eps_vir, vir_row)  12.3 us
    gather x2, local copies, waits for them, and re-layouts, local(): col_energy = jnp.take(eps_occ, occ_col) - jnp.take(eps_vir, vir_col)  9.27 us
    gather x7, other arithmetic, local(): occ_row = jnp.take(slab, rows // V)  7.81 us
    gather x1, local copies, waits for them, and re-layouts, local(): jnp.take(occ_irrep, occ_row)  6.49 us
  transfers between devices with their start and end apart: 2, of which 2 were waited for; matrix products, arithmetic and copies ran while one was open for 26% of the time, Pallas kernels for 0%

commit v1 on v0

v1 whole, which is shorter than its diff:
```python
import jax
import jax.numpy as jnp
from jax import lax
from jax.experimental import pallas as pl
from jax.experimental.pallas import tpu as pltpu
from jax.sharding import PartitionSpec as P

V = 1200
MESH = pl.DeviceIdType.MESH
NX, NY, NZ = 4, 8, 8
AR, BR = 232, 312
AT, BT = 3, 4
KS = 75
KP = 80
KW = 256
M, MP = 900, 912
N, NP = 750, 768
F32, BF16, I32 = jnp.float32, jnp.bfloat16, jnp.int32


def ahead(i, n):
    return i + 2 if 0 < i and i + 2 < n else None


def sends(event):
    kind, i, j = event
    out = []
    if kind == "A":
        if i == 0:
            if j == 0:
                out += [("xL", ("A", 0, 1)), ("xS", ("A", 0, 2))]
            elif j == 1:
                out += [("xL", ("A", 0, 3))]
            out += [("zL", ("A", 1, j)), ("zS", ("A", 2, j))]
        elif ahead(i, NZ):
            out.append(("zL" if i % 2 else "zS", ("A", i + 2, j)))
    elif kind == "B":
        if j == 0:
            if i == 0:
                out += [("zL", ("B", 1, 0)), ("zS", ("B", 2, 0))]
            elif ahead(i, NZ):
                out.append(("zL" if i % 2 else "zS", ("B", i + 2, 0)))
            out += [("xL", ("B", i, 1)), ("xS", ("B", i, 2))]
        elif j == 1:
            out.append(("xL", ("B", i, 3)))
    elif kind == "C" and j == 0:
        if i == 0:
            out += [("yL", ("C", 1, 0)), ("yS", ("C", 2, 0))]
        elif ahead(i, NY):
            out.append(("yL" if i % 2 else "yS", ("C", i + 2, 0)))
        out.append(("core", ("C", i, 1)))
    return out


def arrivals():
    size = {"A": AR * 512, "B": BR * 512, "C": 2 * KP * NP * 4}
    free = {"x": 0.0, "y": 0.0, "z": 0.0, "c": 0.0}
    waiting = [(0.0, 0, ("B", 0, 0)), (0.0, 1, ("A", 0, 0)), (0.0, 2, ("C", 0, 0))]
    count, order = 3, []
    while waiting:
        waiting.sort()
        now, _, event = waiting.pop(0)
        order.append(event)
        for way, new in sends(event):
            axis = way[0]
            rate = 6e5 if axis == "c" else 1e5
            free[axis] = max(free[axis], now) + size[new[0]] / rate
            waiting.append((free[axis] + 1.0, count, new))
            count += 1
    return order


ORDER = arrivals()
OWN = (("B", 0, 0), ("A", 0, 0), ("C", 0, 0))
INDEX = {e: k for k, e in enumerate(e for e in ORDER if e not in OWN)}


def hop(i):
    return jnp.where(lax.rem(i, 2) == 1, (i + 1) // 2, -(i // 2))


def choose(t, values):
    out = jnp.int32(values[0])
    for k, v in enumerate(values[1:], 1):
        out = jnp.where(t == k, jnp.int32(v), out)
    return out


def kernel(lam_ref, cyc_in, ev_ref, eo_ref, oi_ref, slab_ref, pair_ref, start_ref,
           out_ref, bufa, bufb, cyc, lhs, rhs, acc, recip, evs, rowe, tile,
           send_sem, recv_sem):
    row, col = lax.axis_index("row"), lax.axis_index("col")
    y, core = row // 2, lax.rem(row, 2)
    x, z = col // NZ, lax.rem(col, NZ)
    s = 1 - 2 * core

    def xz(dx, dz):
        return (row, lax.rem(x + dx + NX, NX) * NZ + lax.rem(z + dz + NZ, NZ))

    def yc(dy, c):
        return (lax.rem(y + dy + NY, NY) * 2 + c, col)

    target = {
        "xL": xz(s, 0), "xS": xz(-s, 0), "zL": xz(0, s), "zS": xz(0, -s),
        "yL": yc(s, core), "yS": yc(-s, core), "core": yc(0, 1 - core),
    }

    barrier = pltpu.get_barrier_semaphore()
    for where in target.values():
        pl.semaphore_signal(barrier, inc=1, device_id=where, device_id_type=MESH)

    def place(event):
        kind, i, j = event
        return {"A": bufa, "B": bufb, "C": cyc}[kind].at[i, j]

    def copy(way, source, event):
        k = INDEX[event]
        return pltpu.make_async_remote_copy(
            src_ref=place(source), dst_ref=place(event),
            send_sem=send_sem.at[k], recv_sem=recv_sem.at[k],
            device_id=target[way], device_id_type=MESH,
        )

    came = {}
    for event in ORDER:
        for way, new in sends(event):
            came[new] = (way, event)

    def forward(event):
        for way, new in sends(event):
            copy(way, event, new).start()

    lanes = lax.broadcasted_iota(I32, (8, 128), 1)
    bufb[0, 0, 296:312, :] = jnp.zeros((16, 128), F32)
    for t in range(BT):
        bufb[0, 0, t * KS:(t + 1) * KS, :] = lam_ref[:, (AT + t) * 128:(AT + t + 1) * 128]
    tile[...] = jnp.zeros((128, 128), F32)
    tile[0:KS, 0:4] = lam_ref[:, 896:900]
    rem = tile[...].T[0:8, :]
    r80 = pltpu.roll(rem, 80, 1)
    bufb[0, 0, 304:308, :] = jnp.where(lanes < 80, rem, r80)[0:4]
    bufb[0, 0, 308:312, :] = jnp.where(lanes < 32, r80, pltpu.roll(rem, 32, 1))[0:4]
    bufa[0, 0, 224:232, :] = jnp.zeros((8, 128), F32)
    for t in range(AT):
        bufa[0, 0, t * KS:(t + 1) * KS, :] = lam_ref[:, t * 128:(t + 1) * 128]
    cyc[0, 0, :, 72:80, :] = jnp.zeros((2, 8, NP), F32)
    cyc[0, 0, :, :, 640:NP] = jnp.zeros((2, KP, 128), F32)
    for half in range(2):
        cyc[0, 0, half, 0:KS, 0:N] = cyc_in[half * KS:(half + 1) * KS, :]

    pl.semaphore_wait(barrier, 7)
    for event in OWN:
        forward(event)

    def prep_cycle(i, j):
        yy = lax.rem(y - s * hop(jnp.int32(i)) * (1 - 2 * j) + NY, NY)
        cc = core if j == 0 else 1 - core
        for half in range(2):
            c = (yy * 2 + cc) * 2 + half
            xx, zz = c // NZ, lax.rem(c, NZ)
            v = cyc[i, j, half]
            hi = v.astype(BF16)
            lo = (v - hi.astype(F32)).astype(BF16)
            for k, part in enumerate((hi, lo, hi)):
                at = pl.multiple_of(xx * KW + k * KP, 16)
                rhs[zz, pl.ds(at, KP), :] = part

    def stack(v):
        hi = v.astype(BF16).astype(F32)
        lo = v - hi
        pad = jnp.zeros((KW - 3 * KP, 128), F32)
        return jnp.concatenate([hi, hi, lo, pad], axis=0).T.astype(BF16)

    def prep_lam(iz, ix):
        xx = lax.rem(x - s * hop(ix) + NX, NX)
        at = pl.ds(pl.multiple_of(xx * KW, KW), KW)
        for t in range(AT):
            lhs[iz, t * 128:(t + 1) * 128, at] = stack(bufa[iz, ix, t * KS:t * KS + KP, :])
        for t in range(BT):
            m = (AT + t) * 128
            lhs[iz, m:m + 128, at] = stack(bufb[iz, ix, t * KS:t * KS + KP, :])
        v = bufb[iz, ix, 304:312, :]
        hi = v.astype(BF16).astype(F32)
        rows = lax.broadcasted_iota(I32, (8, 128), 0)
        w = jnp.where((rows < 4) | (lanes < 32), hi, v - hi)
        two = jnp.concatenate([w, pltpu.roll(w, 4, 0)], axis=1)
        lhs[iz, 896:912, at] = jnp.concatenate([two, jnp.zeros((8, KW), F32)], axis=0).astype(BF16)

    def prep_many(shards):
        def one(t, carry):
            prep_lam(choose(t, [a for a, _ in shards]), choose(t, [b for _, b in shards]))
            return carry
        lax.fori_loop(0, len(shards), one, 0)

    def irrep_of(index):
        count = jnp.zeros(index.shape, I32)
        for k in range(8):
            count += (index >= start_ref[k]).astype(I32)
        return count - 1

    def scales():
        for zz in range(NZ):
            for xx in range(NX):
                rhs[zz, xx * KW + 3 * KP:(xx + 1) * KW, :] = jnp.zeros((KW - 3 * KP, NP), BF16)
        evs[...] = jnp.zeros((8, 1280), F32)
        evs[:, 0:V] = jnp.broadcast_to(ev_ref[...], (8, V))

        def turned(first, width):
            e = evs[...]
            at = lax.broadcasted_iota(I32, (8, 1280), 1) + first
            r1 = pltpu.roll(e, lax.rem(1280 - first, 1280), 1)
            r2 = pltpu.roll(e, V - first, 1)
            return jnp.where(at < V, r1, r2)[:, 0:width]

        first_row = lax.rem(row * M, V)
        i0 = row * M // V
        i1 = jnp.minimum(i0 + 1, 11)
        s0, s1 = slab_ref[i0], slab_ref[i1]
        first_col = lax.rem(col * N, V)
        j0 = col * N // V
        j1 = jnp.minimum(j0 + 1, 19)
        p0, p1 = pair_ref[j0], pair_ref[j1]

        rv = turned(first_row, 1024)
        at = lax.broadcasted_iota(I32, (8, 1024), 1) + first_row
        rv = jnp.where(at < V, eo_ref[s0], eo_ref[s1]) - rv
        for t in range(8):
            block = jnp.broadcast_to(rv[0:1, t * 128:(t + 1) * 128], (128, 128)).T
            rowe[t * 128:(t + 1) * 128, :] = block

        at = lax.broadcasted_iota(I32, (8, NP), 1) + first_col
        ce = jnp.where(at < V, eo_ref[p0], eo_ref[p1]) - turned(first_col, NP)
        cs = jnp.where(at < V, oi_ref[p0], oi_ref[p1]) ^ irrep_of(jnp.where(at < V, at, at - V))

        def some(k, carry):
            r = pl.multiple_of(k * 16, 16)
            at = lax.broadcasted_iota(I32, (16, 128), 0) + r + first_row
            rs = jnp.where(at < V, oi_ref[s0], oi_ref[s1]) ^ irrep_of(jnp.where(at < V, at, at - V))
            re = rowe[pl.ds(r, 16), :]
            for t in range(NP // 128):
                part = slice(t * 128, (t + 1) * 128)
                denom = re + jnp.broadcast_to(ce[0:1, part], (16, 128))
                same = rs == jnp.broadcast_to(cs[0:1, part], (16, 128))
                recip[pl.ds(r, 16), part] = jnp.where(same, 1.0 / denom, 0.0)
            return carry
        lax.fori_loop(0, MP // 16, some, 0)
        acc[...] = jnp.zeros((MP, NP), F32)

    def multiply(iz):
        zz = lax.rem(z - s * hop(iz) + NZ, NZ)

        def one(n, carry):
            part = pl.ds(pl.multiple_of(n * 256, 256), 256)
            acc[:, part] += jnp.dot(lhs[iz], rhs[zz, :, part], preferred_element_type=F32)
            return carry
        lax.fori_loop(0, NP // 256, one, 0)

    prep_cycle(0, 0)
    scales()

    arrived, ready, done, left = set(), [], [], 16
    arrived.update({("A", 0, 0), ("B", 0, 0)})
    ready.append((0, 0))
    left -= 1
    prepared, multiplied = set(), 0
    for event in ORDER:
        if event in OWN:
            continue
        way, source = came[event]
        copy(way, source, event).wait_recv()
        forward(event)
        kind, i, j = event
        if kind == "C":
            prep_cycle(i, j)
            left -= 1
        else:
            arrived.add(event)
            if ("A", i, j) in arrived and ("B", i, j) in arrived:
                ready.append((i, j))
        if len(ready) >= 2 or len(prepared) + len(ready) == 32 or (ready and left == 0):
            if ready:
                prep_many(ready)
                prepared.update(ready)
                ready = []
        if left == 0:
            first = multiplied
            while multiplied < NZ and all((multiplied, k) in prepared for k in range(NX)):
                multiplied += 1
            if multiplied > first:
                lax.fori_loop(first, multiplied, lambda k, c: (multiply(k), c)[1], 0)

    def finish(k, carry):
        r = pl.ds(pl.multiple_of(k * 48, 8), 48)
        out_ref[r, :] = (acc[r, :] * recip[r, :])[:, 0:N]
        return carry
    lax.fori_loop(0, 18, finish, 0)
    out_ref[864:900, :] = (acc[864:900, :] * recip[864:900, :])[:, 0:N]

    for event, (way, source) in came.items():
        copy(way, source, event).wait_send()


def local(lam, cycle, eps_occ, eps_vir, occ_irrep, slab, pair_occ, irrep_start):
    vmem = pl.BlockSpec(memory_space=pltpu.VMEM)
    smem = pl.BlockSpec(memory_space=pltpu.SMEM)
    return pl.pallas_call(
        kernel,
        out_shape=jax.ShapeDtypeStruct((M, N), F32),
        in_specs=[vmem, vmem, vmem, smem, smem, smem, smem, smem],
        out_specs=vmem,
        scratch_shapes=[
            pltpu.VMEM((NZ, NX, AR, 128), F32),
            pltpu.VMEM((NZ, NX, BR, 128), F32),
            pltpu.VMEM((NY, 2, 2, KP, NP), F32),
            pltpu.VMEM((NZ, MP, NX * KW), BF16),
            pltpu.VMEM((NZ, NX * KW, NP), BF16),
            pltpu.VMEM((MP, NP), F32),
            pltpu.VMEM((MP, NP), F32),
            pltpu.VMEM((8, 1280), F32),
            pltpu.VMEM((1024, 128), F32),
            pltpu.VMEM((128, 128), F32),
            pltpu.SemaphoreType.DMA((len(INDEX),)),
            pltpu.SemaphoreType.DMA((len(INDEX),)),
        ],
        compiler_params=pltpu.CompilerParams(
            collective_id=0, has_side_effects=True, vmem_limit_bytes=62 * 1024 * 1024
        ),
        cost_estimate=pl.CostEstimate(
            flops=2 * 3 * M * N * 2400, bytes_accessed=4 * M * N, transcendentals=0
        ),
    )(lam.T, cycle, eps_vir.reshape(1, V), eps_occ, occ_irrep, slab, pair_occ, irrep_start)


def solution(mesh):
    placed = (P("row", "col"), P("row", "col"), P(), P(), P(), P(), P(), P())
    return jax.shard_map(
        local, mesh=mesh, in_specs=placed, out_specs=P("row", "col"), check_vma=False
    )
```

time: 254 us -> 86.6 us (0.34)
  waiting for transfers between devices: 113 us -> 0 us
  Pallas kernels: 0 us -> 81.5 us
  matrix products: 52.8 us -> 0 us
  local copies, waits for them, and re-layouts: 53.2 us -> 4.8 us
  other arithmetic: 21.1 us -> 0 us
  between operations: 13.6 us -> 0.01 us
    all_gather x2 -> x0, waiting for transfers between devices: 112 us -> none  [the longest x1 110 us: local(): lax.all_gather(lam, 'col', axis=1, tiled=True)]
    pallas_call x0 -> x1, Pallas kernels: none -> 81.5 us  [local(): pl.pallas_call(kernel, out_shape=jax.ShapeDtypeStruct((M, N), F32), in_sp...]
    dot_general x1 -> x0, matrix products: 52.8 us -> none  [local(): jnp.dot(lax.all_gather(lam, 'col', axis=1, tiled=True), cycle_full, preci...]
    gather x9 -> x0, local copies, waits for them, and re-layouts: 38.2 us -> none  [the longest x2 12.3 us: local(): row_energy = jnp.take(eps_occ, occ_row) - jnp.take(eps_vir, vir_row)]
    gather x20 -> x0, other arithmetic: 20.8 us -> none  [the longest x9 12.9 us: local(): occ_col = jnp.take(pair_occ, cols // V)]
    unnamed x10 -> x1, local copies, waits for them, and re-layouts: 15 us -> 3.51 us
  transfers between devices with their start and end apart: 2 -> 0, of which waited for: 2 -> 0; matrix products, arithmetic and copies ran while one was open for 26% -> 0% of each run, Pallas kernels for 0% -> 0%
where the time goes in v1:
time: 86.6 us; the launch traced here: 86.4 us
  Pallas kernels  81.5 us (94%)
  local copies, waits for them, and re-layouts  4.8 us (6%)
    pallas_call x1, Pallas kernels, local(): pl.pallas_call(kernel, out_shape=jax.ShapeDtypeStruct((M, N), F32), in_sp...  81.5 us
    unnamed x1, local copies, waits for them, and re-layouts  3.51 us

profile of v1, /device:TPU:1, one launch (start us, length us, event | category | flops | bytes accessed | tf_op | source)
XLA Modules:
  0.0 86.4 jit_solution(3516257980077937137)
XLA Ops:
  0.0 1.3 %reshape.3.ev_ref = f32[1,1200]{1,0:T(1,128)} reshape(f32[1200]{0:T(1024)} %param.11) | data formatting | bytes 9600 | tf_op jit(solution)/shard_map/reshape | solution.py:331
  1.3 81.5 %shard_map.82 = f32[900,750]{1,0:T(8,128)} custom-call(f32[75,900]{1,0:T(8,128)} %bitcast.1, f32[150,750]{1,0:T(8,128)} %cyc_in.1, f32[1,1200]{1,0:T(1,128)} %reshape.3.ev_ref, f32[200]{0:T(256)} %eo_ref.1, s32[200]{0:T(256)} %oi_ref.1, s32[12]{0:T(128)} %slab_ref.1, s32[20]{0:T(128)} %pair_ref.1, s32[8]{0:T(128)} %start_ref.1), custom_call_target="tpu_custom_call" | custom-call | flops 9720000512 | bytes 2700000 | tf_op jit(solution)/shard_map/pallas_call | solution.py:306
  82.8 3.5 %copy.10 = f32[900,750]{1,0:T(8,128)} copy(f32[900,750]{1,0:T(8,128)} %shard_map.82) | data formatting | bytes 5400000

commit v2 on v0

v2 whole, which is shorter than its diff:
```python
import jax
import jax.numpy as jnp
from jax import lax
from jax.experimental import pallas as pl
from jax.experimental.pallas import tpu as pltpu
from jax.sharding import PartitionSpec as P

V = 1200
MESH = pl.DeviceIdType.MESH
NX, NY, NZ = 4, 8, 8
AR, BR = 216, 320
AT, BT = 3, 4
KA = 72
KS, KP = 75, 80
KW = 256
M, MP = 900, 912
N, NP = 750, 768
F32, BF16, I32 = jnp.float32, jnp.bfloat16, jnp.int32

OWN = (("A", 0, 0, 0), ("B", 0, 0, 0), ("C", 0, 0, 0), ("C", 0, 0, 1))


def source(block):
    kind, i, j, h = block
    if kind == "C" and j == 1:
        return "core", (kind, i, 0, h)
    along_x = j > 0 if kind == "B" else j > 0 and i == 0
    if along_x and kind != "C":
        return ("xL" if j % 2 else "xS"), (kind, i, max(j - 2, 0), h)
    axis = "y" if kind == "C" else "z"
    return axis + ("L" if i % 2 else "S"), (kind, max(i - 2, 0), j, h)


SCHEDULE = (
    (None, (("B", 0, 1, 0), ("C", 1, 0, 0), ("B", 1, 0, 0), ("C", 0, 1, 0), ("B", 0, 2, 0), ("B", 2, 0, 0), ("C", 2, 0, 0), ("A", 0, 1, 0), ("C", 1, 0, 1), ("A", 1, 0, 0), ("C", 0, 1, 1), ("A", 0, 2, 0), ("A", 2, 0, 0), ("C", 2, 0, 1), )),
    (("B", 1, 0, 0), (("B", 1, 1, 0), ("B", 3, 0, 0), ("B", 1, 2, 0), )),
    (("B", 0, 1, 0), (("B", 0, 3, 0), )),
    (("C", 1, 0, 0), (("C", 3, 0, 0), ("C", 1, 1, 0), )),
    (("C", 0, 1, 0), ()),
    (("B", 2, 0, 0), (("B", 2, 1, 0), ("B", 2, 2, 0), ("B", 4, 0, 0), )),
    (("B", 0, 2, 0), ()),
    (("A", 0, 1, 0), (("A", 0, 3, 0), ("A", 1, 1, 0), ("A", 2, 1, 0), )),
    (("A", 1, 0, 0), (("A", 3, 0, 0), )),
    (("C", 2, 0, 0), (("C", 2, 1, 0), ("C", 4, 0, 0), )),
    (("C", 0, 1, 1), ()),
    (("A", 0, 2, 0), (("A", 1, 2, 0), ("A", 2, 2, 0), )),
    (("A", 2, 0, 0), (("A", 4, 0, 0), )),
    (("B", 3, 0, 0), (("B", 3, 1, 0), ("B", 5, 0, 0), ("B", 3, 2, 0), )),
    (("B", 1, 1, 0), (("B", 1, 3, 0), )),
    (("C", 1, 0, 1), (("C", 3, 0, 1), ("C", 1, 1, 1), )),
    (("C", 1, 1, 0), ()),
    (("B", 1, 2, 0), ()),
    (("B", 4, 0, 0), (("B", 4, 1, 0), ("B", 4, 2, 0), ("B", 6, 0, 0), )),
    (("C", 2, 0, 1), (("C", 2, 1, 1), ("C", 4, 0, 1), )),
    (("C", 2, 1, 0), ()),
    (("A", 1, 1, 0), (("A", 3, 1, 0), )),
    (("B", 0, 3, 0), ()),
    (("A", 2, 1, 0), (("A", 4, 1, 0), )),
    (("B", 2, 1, 0), (("B", 2, 3, 0), )),
    (("A", 3, 0, 0), (("A", 5, 0, 0), )),
    (("C", 3, 0, 0), (("C", 5, 0, 0), ("C", 3, 1, 0), )),
    (("C", 1, 1, 1), ()),
    (("A", 1, 2, 0), (("A", 3, 2, 0), )),
    (("B", 2, 2, 0), ()),
    (("A", 2, 2, 0), (("A", 4, 2, 0), )),
    (("C", 4, 0, 0), (("C", 4, 1, 0), ("C", 6, 0, 0), )),
    (("C", 2, 1, 1), ()),
    (("A", 0, 3, 0), (("A", 1, 3, 0), ("A", 2, 3, 0), )),
    (("A", 4, 0, 0), (("A", 6, 0, 0), )),
    (("B", 3, 1, 0), (("B", 3, 3, 0), )),
    (("B", 5, 0, 0), (("B", 5, 1, 0), ("B", 7, 0, 0), ("B", 5, 2, 0), )),
    (("C", 3, 0, 1), (("C", 5, 0, 1), ("C", 3, 1, 1), )),
    (("C", 3, 1, 0), ()),
    (("B", 3, 2, 0), ()),
    (("B", 6, 0, 0), (("B", 6, 1, 0), ("B", 6, 2, 0), )),
    (("C", 4, 0, 1), (("C", 4, 1, 1), ("C", 6, 0, 1), )),
    (("C", 4, 1, 0), ()),
    (("B", 1, 3, 0), ()),
    (("A", 3, 1, 0), (("A", 5, 1, 0), )),
    (("A", 4, 1, 0), (("A", 6, 1, 0), )),
    (("B", 4, 1, 0), (("B", 4, 3, 0), )),
    (("A", 5, 0, 0), (("A", 7, 0, 0), )),
    (("C", 5, 0, 0), (("C", 7, 0, 0), ("C", 5, 1, 0), )),
    (("C", 3, 1, 1), ()),
    (("B", 4, 2, 0), ()),
    (("A", 3, 2, 0), (("A", 5, 2, 0), )),
    (("A", 4, 2, 0), (("A", 6, 2, 0), )),
    (("C", 6, 0, 0), (("C", 6, 1, 0), )),
    (("C", 4, 1, 1), ()),
    (("B", 2, 3, 0), ()),
    (("A", 1, 3, 0), (("A", 3, 3, 0), )),
    (("B", 3, 3, 0), ()),
    (("A", 2, 3, 0), (("A", 4, 3, 0), )),
    (("C", 5, 0, 1), (("C", 7, 0, 1), ("C", 5, 1, 1), )),
    (("C", 5, 1, 0), ()),
    (("A", 6, 0, 0), ()),
    (("B", 5, 1, 0), (("B", 5, 3, 0), )),
    (("B", 7, 0, 0), (("B", 7, 1, 0), ("B", 7, 2, 0), )),
    (("C", 6, 0, 1), (("C", 6, 1, 1), )),
    (("C", 6, 1, 0), ()),
    (("B", 5, 2, 0), ()),
    (("A", 5, 1, 0), (("A", 7, 1, 0), )),
    (("B", 6, 1, 0), (("B", 6, 3, 0), )),
    (("A", 6, 1, 0), ()),
    (("C", 7, 0, 0), (("C", 7, 1, 0), )),
    (("C", 5, 1, 1), ()),
    (("A", 7, 0, 0), ()),
    (("B", 6, 2, 0), ()),
    (("A", 5, 2, 0), (("A", 7, 2, 0), )),
    (("C", 7, 0, 1), (("C", 7, 1, 1), )),
    (("C", 6, 1, 1), ()),
    (("B", 4, 3, 0), ()),
    (("A", 6, 2, 0), ()),
    (("A", 3, 3, 0), (("A", 5, 3, 0), )),
    (("B", 5, 3, 0), ()),
    (("C", 7, 1, 0), ()),
    (("A", 4, 3, 0), (("A", 6, 3, 0), )),
    (("B", 7, 1, 0), (("B", 7, 3, 0), )),
    (("A", 7, 1, 0), ()),
    (("A", 7, 2, 0), ()),
    (("C", 7, 1, 1), ()),
    (("B", 7, 2, 0), ()),
    (("A", 5, 3, 0), (("A", 7, 3, 0), )),
    (("B", 6, 3, 0), ()),
    (("A", 6, 3, 0), ()),
    (("A", 7, 3, 0), ()),
    (("B", 7, 3, 0), ()),
)
BLOCKS = [b for b, _ in SCHEDULE[1:]]
INDEX = {b: k for k, b in enumerate(BLOCKS)}


def hop(i):
    return jnp.where(lax.rem(i, 2) == 1, (i + 1) // 2, -(i // 2))


def place_of(distance, n):
    return jnp.where(distance <= n // 2, jnp.maximum(2 * distance - 1, 0), 2 * (n - distance))


def choose(t, values):
    out = jnp.int32(values[0])
    for k, v in enumerate(values[1:], 1):
        out = jnp.where(t == k, jnp.int32(v), out)
    return out


def gather_kernel(lam_ref, cyc_in, ev_ref, eo_ref, oi_ref, slab_ref, pair_ref, start_ref,
                  acc, recip, bufa, bufb, cyc, lhs, rhs, evs, rowe, tile, send_sem, recv_sem):
    row, col = lax.axis_index("row"), lax.axis_index("col")
    y, core = row // 2, lax.rem(row, 2)
    x, z = col // NZ, lax.rem(col, NZ)
    s = 1 - 2 * core

    def xz(dx, dz):
        return (row, lax.rem(x + dx + NX, NX) * NZ + lax.rem(z + dz + NZ, NZ))

    def yc(dy, c):
        return (lax.rem(y + dy + NY, NY) * 2 + c, col)

    target = {
        "xL": xz(s, 0), "xS": xz(-s, 0), "zL": xz(0, s), "zS": xz(0, -s),
        "yL": yc(s, core), "yS": yc(-s, core), "core": yc(0, 1 - core),
    }

    barrier = pltpu.get_barrier_semaphore()
    for where in target.values():
        pl.semaphore_signal(barrier, inc=1, device_id=where, device_id_type=MESH)

    def ref(block):
        kind, i, j, h = block
        return cyc.at[i, j, h] if kind == "C" else {"A": bufa, "B": bufb}[kind].at[i, j]

    def copy(block):
        way, origin = source(block)
        k = INDEX[block]
        return pltpu.make_async_remote_copy(
            src_ref=ref(origin), dst_ref=ref(block),
            send_sem=send_sem.at[k], recv_sem=recv_sem.at[k],
            device_id=target[way], device_id_type=MESH,
        )

    lanes = lax.broadcasted_iota(I32, (8, 128), 1)
    bufb[0, 0, 296:320, :] = jnp.zeros((24, 128), F32)
    for t in range(BT):
        bufb[0, 0, t * KS:(t + 1) * KS, :] = lam_ref[:, (AT + t) * 128:(AT + t + 1) * 128]
    for t in range(AT):
        bufa[0, 0, t * KA:(t + 1) * KA, :] = lam_ref[0:KA, t * 128:(t + 1) * 128]
        bufb[0, 0, 300 + 3 * t:303 + 3 * t, :] = lam_ref[KA:KS, t * 128:(t + 1) * 128]
    tile[...] = jnp.zeros((128, 128), F32)
    tile[0:KS, 0:4] = lam_ref[:, 896:900]
    rem = tile[...].T[0:8, :]
    r80 = pltpu.roll(rem, 80, 1)
    bufb[0, 0, 312:316, :] = jnp.where(lanes < 80, rem, r80)[0:4]
    bufb[0, 0, 316:320, :] = jnp.where(lanes < 32, r80, pltpu.roll(rem, 32, 1))[0:4]
    cyc[0, 0, :, 72:80, :] = jnp.zeros((2, 8, NP), F32)
    cyc[0, 0, :, :, 640:NP] = jnp.zeros((2, KP, 128), F32)
    for half in range(2):
        cyc[0, 0, half, 0:KS, 0:N] = cyc_in[half * KS:(half + 1) * KS, :]

    pl.semaphore_wait(barrier, 7)
    for block in SCHEDULE[0][1]:
        copy(block).start()

    def cycle_shard(i, j, h):
        yy = lax.rem(y - s * hop(jnp.int32(i)) * (1 - 2 * j) + NY, NY)
        return (yy * 2 + (core if j == 0 else 1 - core)) * 2 + h

    def prep_cycle(i, j, h):
        c = cycle_shard(i, j, h)
        v = cyc[i, j, h]
        hi = v.astype(BF16)
        lo = (v - hi.astype(F32)).astype(BF16)
        for k, part in enumerate((hi, lo, hi)):
            rhs[c, k * KP:(k + 1) * KP, :] = part

    def stack(v):
        hi = v.astype(BF16).astype(F32)
        lo = v - hi
        pad = jnp.zeros((KW - 3 * KP, 128), F32)
        return jnp.concatenate([hi, hi, lo, pad], axis=0).T.astype(BF16)

    def prep_lam(iz, ix):
        t4 = iz * NX + ix
        for t in range(AT):
            v = jnp.concatenate(
                [bufa[iz, ix, t * KA:(t + 1) * KA, :], bufb[iz, ix, 300 + 3 * t:308 + 3 * t, :]], axis=0)
            lhs[t4, t * 128:(t + 1) * 128, :] = stack(v)
        for t in range(BT):
            m = (AT + t) * 128
            lhs[t4, m:m + 128, :] = stack(bufb[iz, ix, t * KS:t * KS + KP, :])
        v = bufb[iz, ix, 312:320, :]
        hi = v.astype(BF16).astype(F32)
        rows = lax.broadcasted_iota(I32, (8, 128), 0)
        w = jnp.where((rows < 4) | (lanes < 32), hi, v - hi)
        two = jnp.concatenate([w, pltpu.roll(w, 4, 0)], axis=1)
        lhs[t4, 896:912, :] = jnp.concatenate([two, jnp.zeros((8, KW), F32)], axis=0).astype(BF16)

    def multiply(t4, c):
        acc[...] += jnp.dot(lhs[t4], rhs[c], preferred_element_type=F32)

    def lam_ready(shards, have):
        def one(t, carry):
            iz, ix = choose(t, [a for a, _ in shards]), choose(t, [b for _, b in shards])
            prep_lam(iz, ix)
            c = lax.rem(x - s * hop(ix) + NX, NX) * NZ + lax.rem(z - s * hop(iz) + NZ, NZ)
            if have == (NY, NY):
                multiply(iz * NX + ix, c)
            else:
                other = (lax.rem(c // 2, 2) != core).astype(I32)
                away = s * (y - c // 4) * (1 - 2 * other)
                near = place_of(lax.rem(away + 2 * NY, NY), NY)

                @pl.when(near < jnp.where(other == 1, have[1], have[0]))
                def _():
                    multiply(iz * NX + ix, c)
            return carry
        lax.fori_loop(0, len(shards), one, 0)

    def cycle_ready(i, j, ready):
        def one(h, carry):
            c = cycle_shard(i, j, h)
            ix = place_of(lax.rem(s * (x - c // NZ) + NX, NX), NX)
            iz = place_of(lax.rem(s * (z - lax.rem(c, NZ)) + NZ, NZ), NZ)

            @pl.when(iz < choose(ix, ready))
            def _():
                multiply(iz * NX + ix, c)
            return carry
        if max(ready):
            lax.fori_loop(0, 2, one, 0)

    def irrep_of(index):
        count = jnp.zeros(index.shape, I32)
        for k in range(8):
            count += (index >= start_ref[k]).astype(I32)
        return count - 1

    def scales():
        for c in range(NX * NZ):
            rhs[c, 3 * KP:KW, :] = jnp.zeros((KW - 3 * KP, NP), BF16)
        evs[...] = jnp.zeros((8, 1280), F32)
        evs[:, 0:V] = jnp.broadcast_to(ev_ref[...].reshape(1, V), (8, V))

        def turned(first, width):
            e = evs[...]
            at = lax.broadcasted_iota(I32, (8, 1280), 1) + first
            r1 = pltpu.roll(e, lax.rem(1280 - first, 1280), 1)
            r2 = pltpu.roll(e, V - first, 1)
            return jnp.where(at < V, r1, r2)[:, 0:width]

        first_row = lax.rem(row * M, V)
        i0 = row * M // V
        s0, s1 = slab_ref[i0], slab_ref[jnp.minimum(i0 + 1, 11)]
        first_col = lax.rem(col * N, V)
        j0 = col * N // V
        p0, p1 = pair_ref[j0], pair_ref[jnp.minimum(j0 + 1, 19)]

        rv = turned(first_row, 1024)
        at = lax.broadcasted_iota(I32, (8, 1024), 1) + first_row
        rv = jnp.where(at < V, eo_ref[s0], eo_ref[s1]) - rv
        for t in range(8):
            rowe[t * 128:(t + 1) * 128, :] = jnp.broadcast_to(rv[0:1, t * 128:(t + 1) * 128], (128, 128)).T

        at = lax.broadcasted_iota(I32, (8, NP), 1) + first_col
        ce = jnp.where(at < V, eo_ref[p0], eo_ref[p1]) - turned(first_col, NP)
        cs = jnp.where(at < V, oi_ref[p0], oi_ref[p1]) ^ irrep_of(jnp.where(at < V, at, at - V))

        def some(k, carry):
            r = pl.multiple_of(k * 16, 16)
            at = lax.broadcasted_iota(I32, (16, 128), 0) + r + first_row
            rs = jnp.where(at < V, oi_ref[s0], oi_ref[s1]) ^ irrep_of(jnp.where(at < V, at, at - V))
            re = rowe[pl.ds(r, 16), :]
            for t in range(NP // 128):
                part = slice(t * 128, (t + 1) * 128)
                denom = re + jnp.broadcast_to(ce[0:1, part], (16, 128))
                same = rs == jnp.broadcast_to(cs[0:1, part], (16, 128))
                recip[pl.ds(r, 16), part] = jnp.where(same, 1.0 / denom, 0.0)
                acc[pl.ds(r, 16), part] = jnp.zeros((16, 128), F32)
            return carry
        lax.fori_loop(0, MP // 16, some, 0)

    prep_cycle(0, 0, 0)
    prep_cycle(0, 0, 1)
    scales()

    arrived = set(OWN)
    have = [1, 0]
    ready = [0] * NX
    waiting = []
    todo = [(0, 0)]
    left = NX * NZ

    def flush():
        nonlocal todo, left
        lam_ready(todo, tuple(have))
        for _, b in todo:
            ready[b] += 1
        left -= len(todo)
        todo = []

    for block, issues in SCHEDULE[1:]:
        copy(block).wait_recv()
        for new in issues:
            copy(new).start()
        arrived.add(block)
        kind, i, j, h = block
        if kind == "C":
            prep_cycle(i, j, h)
            while have[j] < NY and all(("C", have[j], j, k) in arrived for k in range(2)):
                cycle_ready(have[j], j, list(ready))
                have[j] += 1
        else:
            pending = [0] * NX
            for _, b in todo:
                pending[b] += 1
            n = ready[j] + pending[j]
            while n < NZ and {("A", n, j, 0), ("B", n, j, 0)} <= arrived:
                todo.append((n, j))
                n += 1
        if len(todo) >= (2 if left > 4 else 1):
            flush()
    assert not todo and left == 0 and have == [NY, NY]

    for block in BLOCKS:
        copy(block).wait_send()


def scale_kernel(acc, recip, out, stage, sem):
    edges = [0, 152, 304, 456, 608, 760, 900]
    copies = []
    for k in range(6):
        rows = pl.ds(edges[k], edges[k + 1] - edges[k])
        stage[rows, :] = (acc[rows, :] * recip[rows, :])[:, 0:N]
        copies.append(pltpu.make_async_copy(stage.at[rows], out.at[rows], sem.at[k]))
        copies[-1].start()
    for c in copies:
        c.wait()


def local(lam, cycle, eps_occ, eps_vir, occ_irrep, slab, pair_occ, irrep_start):
    vmem = pl.BlockSpec(memory_space=pltpu.VMEM)
    smem = pl.BlockSpec(memory_space=pltpu.SMEM)
    acc, recip = pl.pallas_call(
        gather_kernel,
        out_shape=(pltpu.VMEM((MP, NP), F32), pltpu.VMEM((MP, NP), F32)),
        in_specs=[vmem, vmem, vmem, smem, smem, smem, smem, smem],
        out_specs=(vmem, vmem),
        scratch_shapes=[
            pltpu.VMEM((NZ, NX, AR, 128), F32),
            pltpu.VMEM((NZ, NX, BR, 128), F32),
            pltpu.VMEM((NY, 2, 2, KP, NP), F32),
            pltpu.VMEM((NZ * NX, MP, KW), BF16),
            pltpu.VMEM((NZ * NX, KW, NP), BF16),
            pltpu.VMEM((8, 1280), F32),
            pltpu.VMEM((1024, 128), F32),
            pltpu.VMEM((128, 128), F32),
            pltpu.SemaphoreType.DMA((len(INDEX),)),
            pltpu.SemaphoreType.DMA((len(INDEX),)),
        ],
        compiler_params=pltpu.CompilerParams(
            collective_id=0, has_side_effects=True, vmem_limit_bytes=50 * 1024 * 1024
        ),
        cost_estimate=pl.CostEstimate(
            flops=2 * 3 * M * N * 2400, bytes_accessed=4 * M * N, transcendentals=0
        ),
    )(lam.T, cycle, eps_vir, eps_occ, occ_irrep, slab, pair_occ, irrep_start)
    return pl.pallas_call(
        scale_kernel,
        out_shape=jax.ShapeDtypeStruct((M, N), F32),
        in_specs=[vmem, vmem],
        out_specs=pl.BlockSpec(memory_space=pl.ANY),
        scratch_shapes=[pltpu.VMEM((M, N), F32), pltpu.SemaphoreType.DMA((6,))],
        compiler_params=pltpu.CompilerParams(vmem_limit_bytes=8 * 1024 * 1024),
    )(acc, recip)


def solution(mesh):
    placed = (P("row", "col"), P("row", "col"), P(), P(), P(), P(), P(), P())
    return jax.shard_map(
        local, mesh=mesh, in_specs=placed, out_specs=P("row", "col"), check_vma=False
    )
```

time: 254 us -> 70.1 us (0.28)
  the two profiles are of different devices: /device:TPU:1 before, /device:TPU:2 now
where the time goes in v2:
time: 70.1 us; the launch traced here: 70 us
  Pallas kernels  69.8 us (100%)
    pallas_call x1, Pallas kernels, local(): pl.pallas_call(gather_kernel, out_shape=(pltpu.VMEM((MP, NP), F32), pltpu...  68.2 us
    pallas_call x1, Pallas kernels, local(): pl.pallas_call(scale_kernel, out_shape=jax.ShapeDtypeStruct((M, N), F32),...  1.63 us

profile of v2, /device:TPU:2, one launch (start us, length us, event | category | flops | bytes accessed | tf_op | source)
XLA Modules:
  0.0 70.0 jit_solution(18015212353672950402)
XLA Ops:
  0.0 68.2 %shard_map.82 = (f32[912,768]{1,0:T(8,128)S(1)}, f32[912,768]{1,0:T(8,128)S(1)}) custom-call(f32[75,900]{1,0:T(8,128)} %bitcast.1, f32[150,750]{1,0:T(8,128)} %cyc_in.1, f32[1200]{0:T(1024)} %ev_ref.1, f32[200]{0:T(256)} %eo_ref.1, s32[200]{0:T(256)} %oi_ref.1, s32[12]{0:T(128)} %slab_ref.1, s32[20]{0:T(128)} %pair_ref.1, s32[8]{0:T(128)} %start_ref.1), custom_call_target="tpu_custom_call" | custom-call | flops 9720000512 | bytes 2700000 | tf_op jit(solution)/shard_map/pallas_call | solution.py:384
  68.2 1.6 %shard_map.83 = f32[900,750]{1,0:T(8,128)} custom-call(f32[912,768]{1,0:T(8,128)S(1)} %get-tuple-element.7.acc, f32[912,768]{1,0:T(8,128)S(1)} %get-tuple-element.8.recip), custom_call_target="tpu_custom_call" | custom-call | tf_op jit(solution)/shard_map/pallas_call | solution.py:408

commit v3 on v2

--- a/solution.py
+++ b/solution.py
@@ -220,12 +220,15 @@
         pad = jnp.zeros((KW - 3 * KP, 128), F32)
         return jnp.concatenate([hi, hi, lo, pad], axis=0).T.astype(BF16)
 
-    def prep_lam(iz, ix):
+    def prep_a(iz, ix):
         t4 = iz * NX + ix
         for t in range(AT):
             v = jnp.concatenate(
                 [bufa[iz, ix, t * KA:(t + 1) * KA, :], bufb[iz, ix, 300 + 3 * t:308 + 3 * t, :]], axis=0)
             lhs[t4, t * 128:(t + 1) * 128, :] = stack(v)
+
+    def prep_b(iz, ix):
+        t4 = iz * NX + ix
         for t in range(BT):
             m = (AT + t) * 128
             lhs[t4, m:m + 128, :] = stack(bufb[iz, ix, t * KS:t * KS + KP, :])
@@ -236,38 +239,37 @@
         two = jnp.concatenate([w, pltpu.roll(w, 4, 0)], axis=1)
         lhs[t4, 896:912, :] = jnp.concatenate([two, jnp.zeros((8, KW), F32)], axis=0).astype(BF16)
 
-    def multiply(t4, c):
-        acc[...] += jnp.dot(lhs[t4], rhs[c], preferred_element_type=F32)
-
-    def lam_ready(shards, have):
-        def one(t, carry):
-            iz, ix = choose(t, [a for a, _ in shards]), choose(t, [b for _, b in shards])
-            prep_lam(iz, ix)
-            c = lax.rem(x - s * hop(ix) + NX, NX) * NZ + lax.rem(z - s * hop(iz) + NZ, NZ)
-            if have == (NY, NY):
-                multiply(iz * NX + ix, c)
-            else:
-                other = (lax.rem(c // 2, 2) != core).astype(I32)
-                away = s * (y - c // 4) * (1 - 2 * other)
-                near = place_of(lax.rem(away + 2 * NY, NY), NY)
-
-                @pl.when(near < jnp.where(other == 1, have[1], have[0]))
-                def _():
-                    multiply(iz * NX + ix, c)
-            return carry
-        lax.fori_loop(0, len(shards), one, 0)
+    def multiply(part, t4, c):
+        rows = slice(0, AT * 128) if part == "A" else slice(AT * 128, MP)
+        acc[rows, :] += jnp.dot(lhs[t4, rows, :], rhs[c], preferred_element_type=F32)
+
+    def lam_ready(part, iz, ix, have):
+        iz, ix = jnp.int32(iz), jnp.int32(ix)
+        (prep_a if part == "A" else prep_b)(iz, ix)
+        c = lax.rem(x - s * hop(ix) + NX, NX) * NZ + lax.rem(z - s * hop(iz) + NZ, NZ)
+        if have == (NY, NY):
+            multiply(part, iz * NX + ix, c)
+        else:
+            other = (lax.rem(c // 2, 2) != core).astype(I32)
+            away = s * (y - c // 4) * (1 - 2 * other)
+            near = place_of(lax.rem(away + 2 * NY, NY), NY)
+
+            @pl.when(near < jnp.where(other == 1, have[1], have[0]))
+            def _():
+                multiply(part, iz * NX + ix, c)
 
     def cycle_ready(i, j, ready):
         def one(h, carry):
             c = cycle_shard(i, j, h)
             ix = place_of(lax.rem(s * (x - c // NZ) + NX, NX), NX)
             iz = place_of(lax.rem(s * (z - lax.rem(c, NZ)) + NZ, NZ), NZ)
-
-            @pl.when(iz < choose(ix, ready))
-            def _():
-                multiply(iz * NX + ix, c)
+            for part in "AB":
+                if max(ready[part]):
+                    @pl.when(iz < choose(ix, ready[part]))
+                    def _():
+                        multiply(part, iz * NX + ix, c)
             return carry
-        if max(ready):
+        if max(ready["A"] + ready["B"]):
             lax.fori_loop(0, 2, one, 0)
 
     def irrep_of(index):
@@ -325,19 +327,20 @@
     scales()
 
     arrived = set(OWN)
-    have = [1, 0]
-    ready = [0] * NX
-    waiting = []
-    todo = [(0, 0)]
-    left = NX * NZ
-
-    def flush():
-        nonlocal todo, left
-        lam_ready(todo, tuple(have))
-        for _, b in todo:
-            ready[b] += 1
-        left -= len(todo)
-        todo = []
+    seen, have = [1, 0], [1, 0]
+    here = {"A": [1, 0, 0, 0], "B": [1, 0, 0, 0]}
+    ready = {"A": [0] * NX, "B": [0] * NX}
+    todo = [("B", 0, 0), ("A", 0, 0)]
+
+    def work(most):
+        for kind, i, j in todo[:most]:
+            if kind == "C":
+                cycle_ready(i, j, {k: list(v) for k, v in ready.items()})
+                have[j] += 1
+            else:
+                lam_ready(kind, i, j, tuple(have))
+                ready[kind][j] += 1
+        del todo[:most]
 
     for block, issues in SCHEDULE[1:]:
         copy(block).wait_recv()
@@ -347,20 +350,18 @@
         kind, i, j, h = block
         if kind == "C":
             prep_cycle(i, j, h)
-            while have[j] < NY and all(("C", have[j], j, k) in arrived for k in range(2)):
-                cycle_ready(have[j], j, list(ready))
-                have[j] += 1
+            while seen[j] < NY and all(("C", seen[j], j, k) in arrived for k in range(2)):
+                todo.append(("C", seen[j], j))
+                seen[j] += 1
         else:
-            pending = [0] * NX
-            for _, b in todo:
-                pending[b] += 1
-            n = ready[j] + pending[j]
-            while n < NZ and {("A", n, j, 0), ("B", n, j, 0)} <= arrived:
-                todo.append((n, j))
-                n += 1
-        if len(todo) >= (2 if left > 4 else 1):
-            flush()
-    assert not todo and left == 0 and have == [NY, NY]
+            for part in "BA":
+                n = here[part]
+                while n[j] < NZ and ("B", n[j], j, 0) in arrived and (part, n[j], j, 0) in arrived:
+                    todo.append((part, n[j], j))
+                    n[j] += 1
+        work(1 if len(todo) < 3 else 2)
+    work(len(todo))
+    assert ready == here and have == [NY, NY]
 
     for block in BLOCKS:
         copy(block).wait_send()

time: 70.1 us -> 72.3 us (1.031)
  the two profiles are of different devices: /device:TPU:2 before, /device:TPU:24 now
where the time goes in v3:
time: 72.3 us; the launch traced here: 72.2 us
  Pallas kernels  72 us (100%)
    pallas_call x1, Pallas kernels, local(): pl.pallas_call(gather_kernel, out_shape=(pltpu.VMEM((MP, NP), F32), pltpu...  70.3 us
    pallas_call x1, Pallas kernels, local(): pl.pallas_call(scale_kernel, out_shape=jax.ShapeDtypeStruct((M, N), F32),...  1.63 us

profile of v3, /device:TPU:24, one launch (start us, length us, event | category | flops | bytes accessed | tf_op | source)
XLA Modules:
  0.0 72.2 jit_solution(7229800790282915095)
XLA Ops:
  0.0 70.3 %shard_map.82 = (f32[912,768]{1,0:T(8,128)S(1)}, f32[912,768]{1,0:T(8,128)S(1)}) custom-call(f32[75,900]{1,0:T(8,128)} %bitcast.1, f32[150,750]{1,0:T(8,128)} %cyc_in.1, f32[1200]{0:T(1024)} %ev_ref.1, f32[200]{0:T(256)} %eo_ref.1, s32[200]{0:T(256)} %oi_ref.1, s32[12]{0:T(128)} %slab_ref.1, s32[20]{0:T(128)} %pair_ref.1, s32[8]{0:T(128)} %start_ref.1), custom_call_target="tpu_custom_call" | custom-call | flops 9720000512 | bytes 2700000 | tf_op jit(solution)/shard_map/pallas_call | solution.py:385
  70.3 1.6 %shard_map.83 = f32[900,750]{1,0:T(8,128)} custom-call(f32[912,768]{1,0:T(8,128)S(1)} %get-tuple-element.7.acc, f32[912,768]{1,0:T(8,128)S(1)} %get-tuple-element.8.recip), custom_call_target="tpu_custom_call" | custom-call | tf_op jit(solution)/shard_map/pallas_call | solution.py:409

commit v4 on v3

--- a/solution.py
+++ b/solution.py
@@ -15,6 +15,7 @@
 KW = 256
 M, MP = 900, 912
 N, NP = 750, 768
+LATE = 6
 F32, BF16, I32 = jnp.float32, jnp.bfloat16, jnp.int32
 
 OWN = (("A", 0, 0, 0), ("B", 0, 0, 0), ("C", 0, 0, 0), ("C", 0, 0, 1))
@@ -240,12 +241,15 @@
         lhs[t4, 896:912, :] = jnp.concatenate([two, jnp.zeros((8, KW), F32)], axis=0).astype(BF16)
 
     def multiply(part, t4, c):
-        rows = slice(0, AT * 128) if part == "A" else slice(AT * 128, MP)
+        rows = {"A": slice(0, AT * 128), "B": slice(AT * 128, MP), "AB": slice(0, MP)}[part]
         acc[rows, :] += jnp.dot(lhs[t4, rows, :], rhs[c], preferred_element_type=F32)
 
     def lam_ready(part, iz, ix, have):
         iz, ix = jnp.int32(iz), jnp.int32(ix)
-        (prep_a if part == "A" else prep_b)(iz, ix)
+        if "A" in part:
+            prep_a(iz, ix)
+        if "B" in part:
+            prep_b(iz, ix)
         c = lax.rem(x - s * hop(ix) + NX, NX) * NZ + lax.rem(z - s * hop(iz) + NZ, NZ)
         if have == (NY, NY):
             multiply(part, iz * NX + ix, c)
@@ -263,13 +267,12 @@
             c = cycle_shard(i, j, h)
             ix = place_of(lax.rem(s * (x - c // NZ) + NX, NX), NX)
             iz = place_of(lax.rem(s * (z - lax.rem(c, NZ)) + NZ, NZ), NZ)
-            for part in "AB":
-                if max(ready[part]):
-                    @pl.when(iz < choose(ix, ready[part]))
-                    def _():
-                        multiply(part, iz * NX + ix, c)
+
+            @pl.when(iz < choose(ix, ready))
+            def _():
+                multiply("AB", iz * NX + ix, c)
             return carry
-        if max(ready["A"] + ready["B"]):
+        if max(ready):
             lax.fori_loop(0, 2, one, 0)
 
     def irrep_of(index):
@@ -330,16 +333,19 @@
     seen, have = [1, 0], [1, 0]
     here = {"A": [1, 0, 0, 0], "B": [1, 0, 0, 0]}
     ready = {"A": [0] * NX, "B": [0] * NX}
-    todo = [("B", 0, 0), ("A", 0, 0)]
+    whole = 1
+    todo = [("AB", 0, 0)]
 
     def work(most):
         for kind, i, j in todo[:most]:
             if kind == "C":
-                cycle_ready(i, j, {k: list(v) for k, v in ready.items()})
+                assert ready["A"] == ready["B"]
+                cycle_ready(i, j, list(ready["A"]))
                 have[j] += 1
             else:
                 lam_ready(kind, i, j, tuple(have))
-                ready[kind][j] += 1
+                for part in kind:
+                    ready[part][j] += 1
         del todo[:most]
 
     for block, issues in SCHEDULE[1:]:
@@ -354,14 +360,24 @@
                 todo.append(("C", seen[j], j))
                 seen[j] += 1
         else:
-            for part in "BA":
-                n = here[part]
-                while n[j] < NZ and ("B", n[j], j, 0) in arrived and (part, n[j], j, 0) in arrived:
-                    todo.append((part, n[j], j))
+            late = whole >= NX * NZ - LATE and seen == [NY, NY]
+            if not late:
+                n, m = here["A"], here["B"]
+                while n[j] < NZ and ("A", n[j], j, 0) in arrived and ("B", n[j], j, 0) in arrived:
+                    todo.append(("AB", n[j], j))
                     n[j] += 1
+                    m[j] += 1
+                    whole += 1
+            else:
+                for k in range(NX):
+                    for part in "BA":
+                        n = here[part]
+                        while n[k] < NZ and ("B", n[k], k, 0) in arrived and (part, n[k], k, 0) in arrived:
+                            todo.append((part, n[k], k))
+                            n[k] += 1
         work(1 if len(todo) < 3 else 2)
     work(len(todo))
-    assert ready == here and have == [NY, NY]
+    assert ready == here == {"A": [NZ] * NX, "B": [NZ] * NX} and have == [NY, NY]
 
     for block in BLOCKS:
         copy(block).wait_send()

time: 72.3 us -> 69.5 us (0.961)
  the two profiles are of different devices: /device:TPU:24 before, /device:TPU:4 now
where the time goes in v4:
time: 69.5 us; the launch traced here: 69.3 us
  Pallas kernels  69.1 us (99%)
    pallas_call x1, Pallas kernels, local(): pl.pallas_call(gather_kernel, out_shape=(pltpu.VMEM((MP, NP), F32), pltpu...  67.5 us
    pallas_call x1, Pallas kernels, local(): pl.pallas_call(scale_kernel, out_shape=jax.ShapeDtypeStruct((M, N), F32),...  1.63 us

profile of v4, /device:TPU:4, one launch (start us, length us, event | category | flops | bytes accessed | tf_op | source)
XLA Modules:
  0.0 69.3 jit_solution(18299389345512669744)
XLA Ops:
  0.0 67.5 %shard_map.82 = (f32[912,768]{1,0:T(8,128)S(1)}, f32[912,768]{1,0:T(8,128)S(1)}) custom-call(f32[75,900]{1,0:T(8,128)} %bitcast.1, f32[150,750]{1,0:T(8,128)} %cyc_in.1, f32[1200]{0:T(1024)} %ev_ref.1, f32[200]{0:T(256)} %eo_ref.1, s32[200]{0:T(256)} %oi_ref.1, s32[12]{0:T(128)} %slab_ref.1, s32[20]{0:T(128)} %pair_ref.1, s32[8]{0:T(128)} %start_ref.1), custom_call_target="tpu_custom_call" | custom-call | flops 9720000512 | bytes 2700000 | tf_op jit(solution)/shard_map/pallas_call | solution.py:401
  67.5 1.6 %shard_map.83 = f32[900,750]{1,0:T(8,128)} custom-call(f32[912,768]{1,0:T(8,128)S(1)} %get-tuple-element.7.acc, f32[912,768]{1,0:T(8,128)S(1)} %get-tuple-element.8.recip), custom_call_target="tpu_custom_call" | custom-call | tf_op jit(solution)/shard_map/pallas_call | solution.py:425

commit v5 on v4

--- a/solution.py
+++ b/solution.py
@@ -329,6 +329,7 @@
     prep_cycle(0, 0, 1)
     scales()
 
+    sent = list(SCHEDULE[0][1])
     arrived = set(OWN)
     seen, have = [1, 0], [1, 0]
     here = {"A": [1, 0, 0, 0], "B": [1, 0, 0, 0]}
@@ -352,6 +353,7 @@
         copy(block).wait_recv()
         for new in issues:
             copy(new).start()
+        sent.extend(issues)
         arrived.add(block)
         kind, i, j, h = block
         if kind == "C":
@@ -376,10 +378,12 @@
                             todo.append((part, n[k], k))
                             n[k] += 1
         work(1 if len(todo) < 3 else 2)
+        while len(sent) > 32:
+            copy(sent.pop(0)).wait_send()
     work(len(todo))
     assert ready == here == {"A": [NZ] * NX, "B": [NZ] * NX} and have == [NY, NY]
 
-    for block in BLOCKS:
+    for block in sent:
         copy(block).wait_send()
 
 

time: 69.5 us -> 69.4 us (level)
  no operation moved by 1% of the time
where the time goes in v5:
time: 69.4 us; the launch traced here: 69.2 us
  Pallas kernels  69 us (99%)
    pallas_call x1, Pallas kernels, local(): pl.pallas_call(gather_kernel, out_shape=(pltpu.VMEM((MP, NP), F32), pltpu...  67.4 us
    pallas_call x1, Pallas kernels, local(): pl.pallas_call(scale_kernel, out_shape=jax.ShapeDtypeStruct((M, N), F32),...  1.63 us

profile of v5, /device:TPU:4, one launch (start us, length us, event | category | flops | bytes accessed | tf_op | source)
XLA Modules:
  0.0 69.2 jit_solution(3791600752790233325)
XLA Ops:
  0.0 67.4 %shard_map.82 = (f32[912,768]{1,0:T(8,128)S(1)}, f32[912,768]{1,0:T(8,128)S(1)}) custom-call(f32[75,900]{1,0:T(8,128)} %bitcast.1, f32[150,750]{1,0:T(8,128)} %cyc_in.1, f32[1200]{0:T(1024)} %ev_ref.1, f32[200]{0:T(256)} %eo_ref.1, s32[200]{0:T(256)} %oi_ref.1, s32[12]{0:T(128)} %slab_ref.1, s32[20]{0:T(128)} %pair_ref.1, s32[8]{0:T(128)} %start_ref.1), custom_call_target="tpu_custom_call" | custom-call | flops 9720000512 | bytes 2700000 | tf_op jit(solution)/shard_map/pallas_call | solution.py:405
  67.4 1.6 %shard_map.83 = f32[900,750]{1,0:T(8,128)} custom-call(f32[912,768]{1,0:T(8,128)S(1)} %get-tuple-element.7.acc, f32[912,768]{1,0:T(8,128)S(1)} %get-tuple-element.8.recip), custom_call_target="tpu_custom_call" | custom-call | tf_op jit(solution)/shard_map/pallas_call | solution.py:429
